TPU v7x, 512 devices: a whole 4x8x8 slice. The times are simulated.
512 devices in a mesh: dp: 4 (over x_hi, core), ctx: 128 (over z, x_lo, y).
Axes of the slice: x: 4 (x_hi: 2, x_lo: 2; x = x_hi * 2 + x_lo), y: 8, z: 8, core: 2. Of those that a mesh axis runs over, the one named last changes fastest.
Arguments:
- out_grad: bfloat16 [262144, 4608], P(('dp', 'ctx')), may hold values from -1 to 1
- adapter_inner: bfloat16 [262144, 16], P(('dp', 'ctx')), may hold values from -32 to 32
- doc_lengths: int32 [4, 64], P('dp'), may hold values from 1 to 1536, 65536 in all within a row
- slab_offset: int32 [4], P('dp'), may hold values from 1 to 1535
- included: int32 [4, 64], P('dp'), may hold values 0 or 1
Outputs:
- adapter_second_gradient: float32 [4608, 16], P(('dp', 'ctx'))
- doc_norms: float32 [4, 64], P('dp')
Inputs may be any that keep to these rules, and one draw needn't show every extreme that they name: `doc_lengths`: in each row the lengths sum to 65536, and the largest is exactly 1536.
All inputs are finite; a program needn't handle non-finite values. No bound on the sum of `included` on one device may be relied on, other than what follows from the above.
Results may differ from a plain program's by a relative error of at most 0.0022.
Values may be sent and summed in bfloat16 or wider, within the bound.
A program may use at most 64 MiB of HBM per device.

v0:
```python
import functools

import jax
import jax.numpy as jnp
from jax import lax
from jax.sharding import Mesh
from jax.sharding import PartitionSpec as P

SPAN = 3
CTX = ("ctx_0", "ctx_1", "ctx_2")
DP_CTX = ("dp", "ctx_0", "ctx_1", "ctx_2")


clip_norm = 128.0


def from_behind(block, axis, distance):
    devices = range(lax.axis_size(axis))
    route = [((i - distance) % len(devices), i) for i in devices]
    return lax.ppermute(block, axis, route)


def over_axes(array, axes):
    return functools.reduce(lax.psum, axes, array)


def document_ids(lengths, offset, positions, all_tokens):
    doc_ends = jnp.cumsum(lengths)
    starts = doc_ends - lengths
    longest = jnp.argmax(lengths)
    labels = jnp.arange(lengths.shape[0], dtype=jnp.int32)
    doc_shift = jnp.sum(jnp.where(labels == longest, starts, 0)) + offset
    packed = (positions + doc_shift) % all_tokens
    return jnp.sum((doc_ends[None, :] <= packed[:, None]).astype(jnp.int32), axis=1)


def pair_terms(
    left_ids, left_inner, left_grad, right_ids, right_inner, right_grad, keep_rows, member
):
    inner_gram = jnp.einsum(
        "ir,jr->ij", left_inner, right_inner, preferred_element_type=jnp.float32
    )
    grad_gram = jnp.einsum("id,jd->ij", left_grad, right_grad, preferred_element_type=jnp.float32)
    same_doc = (left_ids[:, None] == right_ids[None, :]) & keep_rows[:, None]
    weight = jnp.sum(jnp.where(same_doc, inner_gram * grad_gram, 0.0), axis=1)
    return jnp.dot(weight, member, precision=lax.Precision.HIGHEST)


def boundary_crossing_plan(
    ids_of, local_document_index, adapter_inner, out_grad, member, my_block, block_rows, all_tokens
):
    first_doc = local_document_index[0]
    last_doc = local_document_index[block_rows - 1]
    before_id = ids_of(jnp.reshape((my_block * block_rows - 1) % all_tokens, (1,)))[0]
    after_id = ids_of(jnp.reshape((my_block + 1) * block_rows % all_tokens, (1,)))[0]
    starts_before = before_id == first_doc
    continues = after_id == last_doc
    crossing = starts_before & (local_document_index == first_doc) | continues & (
        local_document_index == last_doc
    )
    norm_terms = pair_terms(
        local_document_index,
        adapter_inner,
        out_grad,
        local_document_index,
        adapter_inner,
        out_grad,
        jnp.logical_not(crossing),
        member,
    )
    in_first = (local_document_index == first_doc).astype(jnp.bfloat16)
    in_last = (local_document_index == last_doc).astype(jnp.bfloat16)
    first_part = jnp.einsum(
        "tr,td->rd", adapter_inner * in_first[:, None], out_grad, preferred_element_type=jnp.float32
    )
    last_part = jnp.einsum(
        "tr,td->rd", adapter_inner * in_last[:, None], out_grad, preferred_element_type=jnp.float32
    )
    finish = (starts_before & jnp.logical_not((first_doc == last_doc) & continues)).astype(
        jnp.float32
    )
    return (first_doc, last_doc, starts_before, norm_terms, first_part, last_part, finish)


def on_device(out_grad, adapter_inner, doc_lengths, slab_offset, included):
    block_rows = out_grad.shape[0]
    ctx_size = lax.axis_size(CTX)
    my_block = lax.axis_index(CTX)
    all_tokens = ctx_size * block_rows
    lengths = doc_lengths[0]
    doc_count = lengths.shape[0]
    row_index = jnp.arange(block_rows, dtype=jnp.int32)
    labels = jnp.arange(doc_count, dtype=jnp.int32)

    def ids_of(positions):
        return document_ids(lengths, slab_offset[0], positions, all_tokens)

    local_document_index = ids_of(my_block * block_rows + row_index)
    member = (local_document_index[:, None] == labels[None, :]).astype(jnp.float32)
    first_doc, last_doc, starts_before, norm_terms, first_part, last_part, finish = (
        boundary_crossing_plan(
            ids_of,
            local_document_index,
            adapter_inner,
            out_grad,
            member,
            my_block,
            block_rows,
            all_tokens,
        )
    )
    chain_flag = (starts_before & (first_doc == last_doc)).astype(jnp.float32)
    running = last_part
    received = jnp.zeros_like(last_part)
    for distance in range(SPAN):
        received = from_behind(running, CTX, 1)
        running = last_part + chain_flag * received
    complete_document = received + first_part
    end_term = finish * jnp.sum(complete_document * complete_document)
    norm_terms = norm_terms + end_term * (labels == first_doc).astype(jnp.float32)
    squares = over_axes(norm_terms, CTX)
    document_grad_norm = jnp.sqrt(squares)
    clip_factor = (
        included[0].astype(jnp.float32) * clip_norm / jnp.maximum(document_grad_norm, clip_norm)
    )
    token_factor = jnp.dot(member, clip_factor, precision=lax.Precision.HIGHEST)
    scaled = (token_factor[:, None] * adapter_inner.astype(jnp.float32)).astype(jnp.bfloat16)
    adapter_second_gradient = lax.psum_scatter(
        jnp.einsum("td,tr->dr", out_grad, scaled, preferred_element_type=jnp.float32),
        DP_CTX,
        scatter_dimension=0,
        tiled=True,
    )
    return (adapter_second_gradient, document_grad_norm[None, :])


def solution(mesh):
    torus = Mesh(mesh.devices.reshape(mesh.shape["dp"], 8, 2, 8), ("dp", "ctx_0", "ctx_1", "ctx_2"))
    placed = (P(DP_CTX, None), P(DP_CTX, None), P("dp", None), P("dp"), P("dp", None))
    return jax.shard_map(
        on_device,
        mesh=torus,
        in_specs=placed,
        out_specs=(P(DP_CTX, None), P("dp", None)),
        check_vma=False,
    )
```

profile of v0, /device:TPU:1, one launch (start us, length us, event | category | flops | bytes accessed | tf_op | source)
XLA Modules:
  0.0 378.5 jit_solution(4845781089297644548)
XLA Ops:
  7.2 0.0 copy-start
  7.2 0.0 all-reduce.3.cloned.1.call-start
  7.2 1.3 bitcast_reduce_fusion
  8.5 0.7 copy.13
  9.3 0.1 reduce-window.4
  9.4 0.1 reduce.26
  10.2 1.9 fusion.14
  12.8 0.1 convert_reduce_fusion
  12.9 0.6 fusion.25
  13.5 1.3 fusion.23
  14.8 3.1 fusion.9
  17.8 4.0 %collective-permute-start = (f32[16,4608]{1,0:T(8,128)S(1)}, f32[16,4608]{1,0:T(8,128)S(1)}, u32[]{:S(2)}, u32[]{:S(2)}) collective-permute-start(f32[16,4608]{1,0:T(8,128)S(1)} %fusion.9), channel_id=1, source_target_pairs={{127,0},{0,1},{1,2},{2,3},{3,4},{4,5},{5,6},{6,7},{7,8},{8,9},{9,1... | collective-permute-start | bytes 884744 | tf_op jit(solution)/shard_map/ppermute | solution.py:20
  21.9 0.7 convert_reduce_fusion.2
  26.5 0.0 copy-done
  26.5 0.3 fusion.26
  26.9 13.0 %collective-permute-done = f32[16,4608]{1,0:T(8,128)S(1)} collective-permute-done((f32[16,4608]{1,0:T(8,128)S(1)}, f32[16,4608]{1,0:T(8,128)S(1)}, u32[]{:S(2)}, u32[]{:S(2)}) %collective-permute-start) | collective-permute-done | bytes 294944 | tf_op jit(solution)/shard_map/ppermute | solution.py:20
  39.9 1.9 collective-permute-start.1
  41.8 6.6 %fusion.1 = f32[512]{0:T(512)S(1)} fusion(f32[512,512]{0,1:T(8,128)S(1)} %fusion.26, bf16[512,4608]{1,0:T(8,128)(2,1)} %param.5, s32[512]{0:T(512)S(1)} %convert_reduce_fusion, pred[512]{0:T(512)(128)(4,1)S(1)} %or_not_fusion), kind=kOutput, calls=%fused_computation.3 | convolution fusion | flops 2417229312 | bytes 5771776 | tf_op jit(solution)/shard_map/id,jd->ij/dot_general | solution.py:43
  48.4 0.0 copy-start.1
  48.5 4.8 %collective-permute-done.1 = f32[16,4608]{1,0:T(8,128)S(1)} collective-permute-done((f32[16,4608]{1,0:T(8,128)S(1)}, f32[16,4608]{1,0:T(8,128)S(1)}, u32[]{:S(2)}, u32[]{:S(2)}) %collective-permute-start.1) | collective-permute-done | bytes 294944 | tf_op jit(solution)/shard_map/ppermute | solution.py:20
  53.3 1.9 collective-permute-start.2
  55.3 3.1 fusion.7
  58.3 7.5 %collective-permute-done.2 = f32[16,4608]{1,0:T(8,128)S(1)} collective-permute-done((f32[16,4608]{1,0:T(8,128)S(1)}, f32[16,4608]{1,0:T(8,128)S(1)}, u32[]{:S(2)}, u32[]{:S(2)}) %collective-permute-start.2) | collective-permute-done | bytes 294944 | tf_op jit(solution)/shard_map/ppermute | solution.py:20
  65.8 0.7 multiply_reduce_fusion
  67.1 0.9 fusion.2
  68.1 10.7 %psum.21 = f32[64]{0:T(128)S(1)} all-reduce(f32[64]{0:T(128)S(1)} %fusion.2), channel_id=1, replica_groups=mesh['dp'=4,'ctx_0'=8,'ctx_1'=2,'ctx_2'=8] {'ctx_0'}, use_global_device_ids=true, to_apply=%region_8.9 | all-reduce | flops 64 | bytes 512 | tf_op jit(solution)/shard_map/psum | solution.py:24
  78.7 4.1 %psum.22 = f32[64]{0:T(128)S(1)} all-reduce(f32[64]{0:T(128)S(1)} %psum.21), channel_id=1, replica_groups=mesh['dp'=4,'ctx_0'=8,'ctx_1'=2,'ctx_2'=8] {'ctx_1'}, use_global_device_ids=true, to_apply=%region_9.10 | all-reduce | flops 64 | bytes 512 | tf_op jit(solution)/shard_map/psum | solution.py:24
  82.8 10.7 %psum.23 = f32[64]{0:T(128)S(1)} all-reduce(f32[64]{0:T(128)S(1)} %psum.22), channel_id=1, replica_groups=mesh['dp'=4,'ctx_0'=8,'ctx_1'=2,'ctx_2'=8] {'ctx_2'}, use_global_device_ids=true, to_apply=%region_10.11 | all-reduce | flops 64 | bytes 512 | tf_op jit(solution)/shard_map/psum | solution.py:24
  93.5 0.0 copy-done.1
  93.5 0.3 fusion.3
  93.8 3.8 %convolution_bitcast_fusion = f32[4608,16]{0,1:T(8,128)} fusion(bf16[512,4608]{1,0:T(8,128)(2,1)} %param.5, bf16[512,16]{0,1:T(8,128)(2,1)S(1)} %copy-done, f32[512]{0:T(512)S(1)} %bitcast.42), kind=kOutput, calls=%fused_computation | convolution fusion | flops 75522048 | bytes 5031936 | tf_op jit(solution)/shard_map/td,tr->dr/dot_general | solution.py:129
  97.6 0.0 all-reduce.3.cloned.1.call-update
  97.6 0.5 sqrt_bitcast_fusion
  98.1 272.1 %all-reduce.3.cloned.1.call-done = f32[4608,16]{0,1:T(8,128)} async-done(((f32[4608,16]{0,1:T(8,128)}), f32[4608,16]{0,1:T(8,128)}) %all-reduce.3.cloned.1.call-update) | async-done | bytes 294928
  370.2 0.8 constant_dynamic-slice_fusion
  371.0 0.7 copy.14
  (4 shorter events, 0.1 us)
Async XLA Ops:
  7.2 19.4 %copy-start = (bf16[512,16]{0,1:T(8,128)(2,1)S(1)}, bf16[512,16]{0,1:T(8,128)(2,1)}, u32[]{:S(2)}) copy-start(bf16[512,16]{0,1:T(8,128)(2,1)} %param.6) | copy-start | bytes 49156
  7.2 363.0 %all-reduce.3.cloned.1.call-start = ((), (), s32[]{:S(2)}) async-start(), calls=%async_computation | async-start | bytes 589824
  17.8 22.1 %collective-permute-start = (f32[16,4608]{1,0:T(8,128)S(1)}, f32[16,4608]{1,0:T(8,128)S(1)}, u32[]{:S(2)}, u32[]{:S(2)}) collective-permute-start(f32[16,4608]{1,0:T(8,128)S(1)} %fusion.9), channel_id=1, source_target_pairs={{127,0},{0,1},{1,2},{2,3},{3,4},{4,5},{5,6},{6,7},{7,8},{8,9},{9,1... | collective-permute-start | bytes 884744 | tf_op jit(solution)/shard_map/ppermute | solution.py:20
  39.9 13.4 %collective-permute-start.1 = (f32[16,4608]{1,0:T(8,128)S(1)}, f32[16,4608]{1,0:T(8,128)S(1)}, u32[]{:S(2)}, u32[]{:S(2)}) collective-permute-start(f32[16,4608]{1,0:T(8,128)S(1)} %multiply_add_fusion.1), channel_id=1, source_target_pairs={{127,0},{0,1},{1,2},{2,3},{3,4},{4,5},{5,6},{6,7},{7,8},{8,9},{9,1... | collective-permute-start | bytes 884744 | tf_op jit(solution)/shard_map/ppermute | solution.py:20
  48.4 45.0 %copy-start.1 = (s32[1,64]{1,0:T(1,128)S(1)}, s32[1,64]{1,0:T(1,128)}, u32[]{:S(2)}) copy-start(s32[1,64]{1,0:T(1,128)} %param.9) | copy-start | bytes 772
  53.3 12.5 %collective-permute-start.2 = (f32[16,4608]{1,0:T(8,128)S(1)}, f32[16,4608]{1,0:T(8,128)S(1)}, u32[]{:S(2)}, u32[]{:S(2)}) collective-permute-start(f32[16,4608]{1,0:T(8,128)S(1)} %multiply_add_fusion), channel_id=1, source_target_pairs={{127,0},{0,1},{1,2},{2,3},{3,4},{4,5},{5,6},{6,7},{7,8},{8,9},{9,1... | collective-permute-start | bytes 884744 | tf_op jit(solution)/shard_map/ppermute | solution.py:20
Sparse Core Ops, SparseCore 0:
  97.7 272.4 all-reduce.2
where the time goes:
time: 379 us
  waiting for transfers between devices  297 us (78%)
  blocking collectives  25.4 us (7%)
  between operations  20.1 us (5%)
  matrix products  18.1 us (5%)
  starting transfers between devices  7.92 us (2%)
  other arithmetic  6.31 us (2%)
    unnamed x2, waiting for transfers between devices  272 us
    psum x3, blocking collectives, over_axes(): return functools.reduce(lax.psum, axes, array)  25.4 us
    ppermute x3, waiting for transfers between devices, from_behind(): return lax.ppermute(block, axis, route)  25.3 us
    ppermute x3, starting transfers between devices, from_behind(): return lax.ppermute(block, axis, route)  7.88 us
  transfers between devices with their start and end apart: 4, of which 4 were waited for; matrix products, arithmetic and copies ran while one was open for 3% of the time, Pallas kernels for 0%

commit v1 on v0

v1 whole, which is shorter than its diff:
```python
import functools

import jax
import jax.numpy as jnp
from jax import lax
from jax.experimental import pallas as pl
from jax.experimental.pallas import tpu as pltpu
from jax.sharding import PartitionSpec as P

CLIP_NORM = 128.0
LONGEST = 1536.0
LOCAL_DOCS = 23
REACH = 3
PARTS = 4
MESH = pl.DeviceIdType.MESH
F32 = jnp.float32
BF16 = jnp.bfloat16


def lane_tiles(array):
    return [array[:, k : k + 128] for k in range(0, array.shape[1], 128)]


def kernel(
    geometry, grad_hbm, inner_ref, len_ref, off_ref, inc_ref,
    out_ref, norm_ref,
    grad, lhs, last_out, first_out, last_in, first_in, last_far, first_far,
    terms_out, terms_in, clipped, send_1, recv_1, send_2, recv_2, send_3, recv_3,
    load_sem, halo_send, halo_recv, terms_send, terms_recv,
    send_sem_1, recv_sem_1, send_sem_2, recv_sem_2, send_sem_3, recv_sem_3,
):
    n_dp, n_z, n_x, n_y = geometry
    n_ctx = n_z * n_x * n_y
    rows, width = grad.shape
    rank = inner_ref.shape[0]
    docs = len_ref.shape[1]
    part = width // PARTS
    tokens = n_ctx * rows
    dp = lax.axis_index("dp")
    block = lax.axis_index("ctx")
    z, x, y = block // (n_x * n_y), (block // n_y) % n_x, block % n_y
    n_group = n_dp * n_x
    group = dp * n_x + x

    def along(distance):
        return (dp, lax.rem(block + distance + n_ctx, n_ctx))

    def in_group(g):
        return (g // n_x, z * (n_x * n_y) + lax.rem(g, n_x) * n_y + y)

    def in_z(other):
        return (dp, other * (n_x * n_y) + x * n_y + y)

    def in_y(other):
        return (dp, z * (n_x * n_y) + x * n_y + other)

    loads = []
    for p in range(PARTS):
        columns = pl.ds(p * part, part)
        loads.append(
            pltpu.make_async_copy(grad_hbm.at[:, columns], grad.at[:, columns], load_sem.at[p])
        )
        loads[-1].start()

    barrier = pltpu.get_barrier_semaphore()
    greeted = 0
    for distance in range(1, REACH + 1):
        for sign in (1, -1):
            pl.semaphore_signal(
                barrier, inc=1, device_id=along(sign * distance), device_id_type=MESH
            )
            greeted += 1
    for size, me, where in ((n_group, group, in_group), (n_z, z, in_z), (n_y, y, in_y)):
        for step in range(1, size):
            pl.semaphore_signal(
                barrier, inc=1, device_id=where(lax.rem(me + step, size)), device_id_type=MESH
            )
            greeted += 1

    lengths = len_ref[...].astype(F32)
    down = lax.broadcasted_iota(jnp.int32, (docs, docs), 0)
    across = lax.broadcasted_iota(jnp.int32, (docs, docs), 1)
    own = down == across
    spread = jnp.broadcast_to(lengths, (docs, docs))
    ends = jnp.sum(jnp.where(across <= down, spread, 0.0), axis=1, keepdims=True)
    length = jnp.sum(jnp.where(own, spread, 0.0), axis=1, keepdims=True)
    start = jnp.min(
        jnp.where(length == LONGEST, ends - length, float(tokens)), axis=0, keepdims=True
    )
    shift = start + off_ref[0].astype(F32)

    def ids_of(positions):
        packed = positions.astype(F32) + shift
        packed = jnp.where(packed >= tokens, packed - tokens, packed)
        return jnp.sum(jnp.where(ends <= packed, 1.0, 0.0), axis=0, keepdims=True)

    ids = ids_of(block * rows + lax.broadcasted_iota(jnp.int32, (1, rows), 1))
    lane = lax.broadcasted_iota(jnp.int32, (1, 128), 1)
    places = jnp.zeros((1, 128), jnp.int32)
    offsets = (-rows - 1, -1, 0, rows, 2 * rows, rows - 1)
    for i, offset in enumerate(offsets):
        places = jnp.where(lane == i, offset, places)
    places = places + block * rows
    places = jnp.where(places < 0, places + tokens, places)
    places = jnp.where(places >= tokens, places - tokens, places)
    edge_ids = ids_of(places)
    behind_2, behind_1, first, ahead_1, ahead_2, last = [
        jnp.sum(jnp.where(lane == i, edge_ids, 0.0), axis=1, keepdims=True)
        for i in range(len(offsets))
    ]

    inner = inner_ref[...].astype(F32)
    local = ids - first
    local = jnp.where(local < 0.0, local + docs, local)
    lhs[0:rank, :] = jnp.where(ids == last, inner, 0.0).astype(BF16)
    for q in range(LOCAL_DOCS):
        lhs[(q + 1) * rank : (q + 2) * rank, :] = jnp.where(local == float(q), inner, 0.0).astype(
            BF16
        )

    def halo(p):
        columns = pl.ds(p * part, part)
        far = pl.ds((p % (PARTS // 2)) * part, part)
        low = p < PARTS // 2
        moves = [
            (last_out.at[:, columns], last_in.at[:, columns], along(1)),
            (first_out.at[:, columns], first_in.at[:, columns], along(-1)),
            (last_out.at[:, columns], last_far.at[:, far], along(2))
            if low
            else (first_out.at[:, columns], first_far.at[:, far], along(-2)),
        ]
        return [
            pltpu.make_async_remote_copy(
                src_ref=src,
                dst_ref=dst,
                send_sem=halo_send.at[p, i],
                recv_sem=halo_recv.at[p, i],
                device_id=to,
                device_id_type=MESH,
            )
            for i, (src, dst, to) in enumerate(moves)
        ]

    doc_rows = LOCAL_DOCS * rank
    squares = jnp.zeros((doc_rows, 128), F32)
    halos = []
    for p in range(PARTS):
        loads[p].wait()
        columns = slice(p * part, (p + 1) * part)
        sums = jnp.dot(lhs[...], grad[:, columns], preferred_element_type=F32)
        last_out[:, columns] = sums[0:rank].astype(BF16)
        first_out[:, columns] = sums[rank : 2 * rank].astype(BF16)
        if p == 0:
            pl.semaphore_wait(barrier, greeted)
        halos.append(halo(p))
        for copy in halos[-1]:
            copy.start()
        for tile in lane_tiles(sums[rank:]):
            squares = squares + tile * tile

    by_row = jnp.sum(squares, axis=1, keepdims=True)
    label = first + lax.shift_right_logical(
        lax.broadcasted_iota(jnp.int32, (doc_rows, 1), 0), rank.bit_length() - 1
    ).astype(F32)
    label = jnp.where(label >= docs, label - docs, label)
    lane_f = lane.astype(F32)
    terms = jnp.sum(jnp.where(label == lane_f, by_row, 0.0), axis=0, keepdims=True)

    def flag(condition):
        return jnp.where(condition, 2.0, 0.0)

    pair_1 = flag(behind_1 == first)
    pair_2 = flag(behind_1 == ahead_1)
    pair_3_ahead = flag(behind_1 == ahead_2)
    pair_3_behind = flag(behind_2 == ahead_1)
    crossed = jnp.zeros((rank, 128), F32)
    for p in range(PARTS):
        columns = slice(p * part, (p + 1) * part)
        far = slice((p % (PARTS // 2)) * part, (p % (PARTS // 2) + 1) * part)
        for copy in halos[p]:
            copy.wait_recv()
        from_behind = last_in[:, columns].astype(F32)
        from_ahead = first_in[:, columns].astype(F32)
        partner = pair_1 * first_out[:, columns].astype(F32) + pair_2 * from_ahead
        if p < PARTS // 2:
            product = from_behind * partner + (pair_3_behind * from_ahead) * last_far[
                :, far
            ].astype(F32)
        else:
            product = from_behind * (partner + pair_3_ahead * first_far[:, far].astype(F32))
        for tile in lane_tiles(product):
            crossed = crossed + tile
    cross = jnp.sum(jnp.sum(crossed, axis=1, keepdims=True), axis=0, keepdims=True)
    terms = terms + jnp.where(lane_f == first, cross, 0.0)

    terms_out[...] = jnp.broadcast_to(terms, (8, 128))
    news = []
    for distance in range(1, REACH + 1):
        for sign in (1, -1):
            slot = len(news)
            news.append(
                pltpu.make_async_remote_copy(
                    src_ref=terms_out,
                    dst_ref=terms_in.at[slot],
                    send_sem=terms_send.at[slot],
                    recv_sem=terms_recv.at[slot],
                    device_id=along(sign * distance),
                    device_id_type=MESH,
                )
            )
            news[-1].start()
    near = terms
    for slot, copy in enumerate(news):
        copy.wait_recv()
        near = near + terms_in[slot, 0:1, :]

    norms = jnp.sqrt(jnp.maximum(near[:, 0:docs], 0.0))
    factor = inc_ref[...].astype(F32) * CLIP_NORM / jnp.maximum(norms, CLIP_NORM)
    factor = jnp.sum(jnp.where(own, jnp.broadcast_to(factor, (docs, docs)), 0.0), axis=1, keepdims=True)
    name = lax.broadcasted_iota(jnp.int32, (docs, 1), 0).astype(F32)
    token_factor = jnp.sum(jnp.where(ids == name, factor, 0.0), axis=0, keepdims=True)
    scaled = (token_factor * inner).astype(BF16)
    for p in range(PARTS):
        columns = slice(p * part, (p + 1) * part)
        clipped[:, columns] = jnp.dot(scaled, grad[:, columns], preferred_element_type=F32)

    each = width // (n_dp * n_ctx)
    run = n_y * each
    half = n_z * run
    for g in range(n_group):
        base = (g // n_x) * (n_ctx * each) + (g % n_x) * run
        for k in range(n_z):
            column = base + k * (n_x * run)
            send_1[g, :, k * run : (k + 1) * run] = clipped[0:8, column : column + run]
            send_1[g, :, half + k * run : half + (k + 1) * run] = clipped[8:16, column : column + run]
        send_1[g, :, 2 * half : 2 * half + 128] = jnp.broadcast_to(terms, (8, 128))

    def exchange(size, me, where, out, into, out_sem, in_sem):
        copies = []
        for step in range(1, size):
            to = lax.rem(me + step, size)
            copies.append(
                pltpu.make_async_remote_copy(
                    src_ref=out.at[to],
                    dst_ref=into.at[me],
                    send_sem=out_sem.at[step],
                    recv_sem=in_sem.at[me],
                    device_id=where(to),
                    device_id_type=MESH,
                )
            )
            copies[-1].start()
        into[me] = out[me]
        for step in range(1, size):
            source = lax.rem(me + size - step, size)
            pltpu.make_async_remote_copy(
                src_ref=out.at[source],
                dst_ref=into.at[source],
                send_sem=out_sem.at[step],
                recv_sem=in_sem.at[source],
                device_id=where(source),
                device_id_type=MESH,
            ).wait_recv()
        return copies

    sent = exchange(n_group, group, in_group, send_1, recv_1, send_sem_1, recv_sem_1)
    total = recv_1[0, :, 0 : 2 * half]
    for g in range(1, n_group):
        total = total + recv_1[g, :, 0 : 2 * half]
    all_terms = recv_1[dp * n_x, :, 2 * half : 2 * half + 128]
    for k in range(1, n_x):
        all_terms = all_terms + recv_1[dp * n_x + k, :, 2 * half : 2 * half + 128]
    for k in range(n_z):
        send_2[k, 0:8, 0:run] = total[:, k * run : (k + 1) * run]
        send_2[k, 8:16, 0:run] = total[:, half + k * run : half + (k + 1) * run]
        send_2[k, 16:24, :] = all_terms
    sent += exchange(n_z, z, in_z, send_2, recv_2, send_sem_2, recv_sem_2)
    total = recv_2[0, 0:16, 0:run]
    all_terms = recv_2[0, 16:24, :]
    for k in range(1, n_z):
        total = total + recv_2[k, 0:16, 0:run]
        all_terms = all_terms + recv_2[k, 16:24, :]
    for k in range(n_y):
        send_3[k, 0:16, 0:each] = total[:, k * each : (k + 1) * each]
        send_3[k, 16:24, :] = all_terms
    sent += exchange(n_y, y, in_y, send_3, recv_3, send_sem_3, recv_sem_3)
    total = recv_3[0, 0:16, 0:each]
    all_terms = recv_3[0, 16:17, 0:docs]
    for k in range(1, n_y):
        total = total + recv_3[k, 0:16, 0:each]
        all_terms = all_terms + recv_3[k, 16:17, 0:docs]
    out_ref[...] = total
    norm_ref[...] = jnp.sqrt(jnp.maximum(all_terms, 0.0))

    for copies in halos:
        for copy in copies:
            copy.wait_send()
    for copy in news + sent:
        copy.wait_send()


def on_device(geometry, out_grad, adapter_inner, doc_lengths, slab_offset, included):
    n_dp, n_z, n_x, n_y = geometry
    n_group = n_dp * n_x
    rows, width = out_grad.shape
    rank = adapter_inner.shape[1]
    docs = doc_lengths.shape[1]
    each = width // (n_dp * n_z * n_x * n_y)
    depth = (LOCAL_DOCS + 1) * rank
    long = 2 * n_z * n_y * each + 128
    in_vmem = pl.BlockSpec(memory_space=pltpu.VMEM)
    dma = pltpu.SemaphoreType.DMA
    gradient, norms = pl.pallas_call(
        functools.partial(kernel, geometry),
        out_shape=(
            jax.ShapeDtypeStruct((rank, each), F32),
            jax.ShapeDtypeStruct((1, docs), F32),
        ),
        in_specs=[
            pl.BlockSpec(memory_space=pl.ANY),
            in_vmem,
            in_vmem,
            pl.BlockSpec(memory_space=pltpu.SMEM),
            in_vmem,
        ],
        out_specs=(in_vmem, in_vmem),
        scratch_shapes=[
            pltpu.VMEM((rows, width), BF16),
            pltpu.VMEM((depth, rows), BF16),
            pltpu.VMEM((rank, width), BF16),
            pltpu.VMEM((rank, width), BF16),
            pltpu.VMEM((rank, width), BF16),
            pltpu.VMEM((rank, width), BF16),
            pltpu.VMEM((rank, width // 2), BF16),
            pltpu.VMEM((rank, width // 2), BF16),
            pltpu.VMEM((8, 128), F32),
            pltpu.VMEM((2 * REACH, 8, 128), F32),
            pltpu.VMEM((rank, width), F32),
            pltpu.VMEM((n_group, 8, long), F32),
            pltpu.VMEM((n_group, 8, long), F32),
            pltpu.VMEM((n_z, 24, 128), F32),
            pltpu.VMEM((n_z, 24, 128), F32),
            pltpu.VMEM((n_y, 24, 128), F32),
            pltpu.VMEM((n_y, 24, 128), F32),
            dma((PARTS,)),
            dma((PARTS, 3)),
            dma((PARTS, 3)),
            dma((2 * REACH,)),
            dma((2 * REACH,)),
            dma((n_group,)),
            dma((n_group,)),
            dma((n_z,)),
            dma((n_z,)),
            dma((n_y,)),
            dma((n_y,)),
        ],
        compiler_params=pltpu.CompilerParams(
            collective_id=0, has_side_effects=True, vmem_limit_bytes=40 * 2**20
        ),
    )(out_grad, adapter_inner.T, doc_lengths, slab_offset, included)
    return gradient.T, norms


def solution(mesh):
    n_x, n_y = 2, 8
    geometry = (mesh.shape["dp"], mesh.shape["ctx"] // (n_x * n_y), n_x, n_y)
    placed = (P(("dp", "ctx"), None), P(("dp", "ctx"), None), P("dp", None), P("dp"), P("dp", None))
    return jax.shard_map(
        functools.partial(on_device, geometry),
        mesh=mesh,
        in_specs=placed,
        out_specs=(P(("dp", "ctx"), None), P("dp", None)),
        check_vma=False,
    )
```

time: 379 us -> 53.9 us (0.14)
  waiting for transfers between devices: 297 us -> 0 us
  Pallas kernels: 0 us -> 46.9 us
  blocking collectives: 25.4 us -> 0 us
  between operations: 20.1 us -> 1.3 us
  matrix products: 18.1 us -> 0 us
  starting transfers between devices: 7.92 us -> 0 us
  other arithmetic: 6.31 us -> 0 us
    unnamed x2 -> x0, waiting for transfers between devices: 272 us -> none
    pallas_call x0 -> x1, Pallas kernels: none -> 46.9 us  [on_device(): pl.pallas_call(functools.partial(kernel, geometry), out_shape=(jax.ShapeD...]
    psum x3 -> x0, blocking collectives: 25.4 us -> none  [over_axes(): return functools.reduce(lax.psum, axes, array)]
    ppermute x3 -> x0, waiting for transfers between devices: 25.3 us -> none  [from_behind(): return lax.ppermute(block, axis, route)]
    dot_general x7 -> x0, matrix products: 18.1 us -> none  [the longest x1 6.59 us: pair_terms(): jnp.einsum('id,jd->ij', left_grad, right_grad, preferred_element_type=jnp...]
    ppermute x3 -> x0, starting transfers between devices: 7.88 us -> none  [from_behind(): return lax.ppermute(block, axis, route)]
    unnamed x6 -> x10, local copies, waits for them, and re-layouts: 1.48 us -> 5.54 us
  transfers between devices with their start and end apart: 4 -> 0, of which waited for: 4 -> 0; matrix products, arithmetic and copies ran while one was open for 3% -> 0% of each run, Pallas kernels for 0% -> 0%
where the time goes in v1:
time: 53.9 us; the launch traced here: 53.7 us
  Pallas kernels  46.9 us (87%)
  local copies, waits for them, and re-layouts  5.54 us (10%)
  between operations  1.3 us (2%)
    pallas_call x1, Pallas kernels, on_device(): pl.pallas_call(functools.partial(kernel, geometry), out_shape=(jax.ShapeD...  46.9 us
    unnamed x10, local copies, waits for them, and re-layouts  5.54 us

profile of v1, /device:TPU:1, one launch (start us, length us, event | category | flops | bytes accessed | tf_op | source)
XLA Modules:
  0.0 53.7 jit_solution(1843944189547411341)
XLA Ops:
  1.3 0.0 copy-start
  1.3 2.3 %copy-done = bf16[512,4608]{1,0:T(8,128)(2,1)S(1)} copy-done((bf16[512,4608]{1,0:T(8,128)(2,1)S(1)}, bf16[512,4608]{1,0:T(8,128)(2,1)}, u32[]{:S(2)}) %copy-start) | copy-done | bytes 4718616
  3.6 0.0 copy-start.1
  3.6 0.7 %copy-done.1 = bf16[512,16]{0,1:T(8,128)(2,1)S(1)} copy-done((bf16[512,16]{0,1:T(8,128)(2,1)S(1)}, bf16[512,16]{0,1:T(8,128)(2,1)}, u32[]{:S(2)}) %copy-start.1) | copy-done | bytes 16408
  4.3 0.0 copy-start.2
  4.3 0.7 %copy-done.2 = s32[1,64]{1,0:T(1,128)S(1)} copy-done((s32[1,64]{1,0:T(1,128)S(1)}, s32[1,64]{1,0:T(1,128)}, u32[]{:S(2)}) %copy-start.2) | copy-done | bytes 280
  5.0 0.0 copy-start.3
  5.0 0.7 %copy-done.3 = s32[1,64]{1,0:T(1,128)S(1)} copy-done((s32[1,64]{1,0:T(1,128)S(1)}, s32[1,64]{1,0:T(1,128)}, u32[]{:S(2)}) %copy-start.3) | copy-done | bytes 280
  5.6 46.9 %shard_map.68 = (f32[16,9]{1,0:T(8,128)S(1)}, f32[1,64]{1,0:T(1,128)S(1)}) custom-call(bf16[512,4608]{1,0:T(8,128)(2,1)S(1)} %copy-done, bf16[16,512]{1,0:T(8,128)(2,1)S(1)} %bitcast.2, s32[1,64]{1,0:T(1,128)S(1)} %copy-done.2, s32[1]{0:T(128)S(6)} %copy.9.off_ref, s32[1,64]{1,0:T(1,128)S(1)} %copy-done.3), custom_call_target="tpu_custom_call" | custom-call | tf_op jit(solution)/shard_map/pallas_call | solution.py:313
  52.5 0.7 %copy.7 = f32[9,16]{1,0:T(8,128)} copy(f32[9,16]{0,1:T(8,128)S(1)} %bitcast.3) | data formatting | bytes 1152
  53.2 0.5 copy.10
Async XLA Ops:
  1.3 2.3 %copy-start = (bf16[512,4608]{1,0:T(8,128)(2,1)S(1)}, bf16[512,4608]{1,0:T(8,128)(2,1)}, u32[]{:S(2)}) copy-start(bf16[512,4608]{1,0:T(8,128)(2,1)} %grad_hbm.1) | copy-start | bytes 14155780
  3.6 0.7 %copy-start.1 = (bf16[512,16]{0,1:T(8,128)(2,1)S(1)}, bf16[512,16]{0,1:T(8,128)(2,1)}, u32[]{:S(2)}) copy-start(bf16[512,16]{0,1:T(8,128)(2,1)} %param.6) | copy-start | bytes 49156
  4.3 0.7 %copy-start.2 = (s32[1,64]{1,0:T(1,128)S(1)}, s32[1,64]{1,0:T(1,128)}, u32[]{:S(2)}) copy-start(s32[1,64]{1,0:T(1,128)} %len_ref.1) | copy-start | bytes 772
  5.0 0.7 %copy-start.3 = (s32[1,64]{1,0:T(1,128)S(1)}, s32[1,64]{1,0:T(1,128)}, u32[]{:S(2)}) copy-start(s32[1,64]{1,0:T(1,128)} %inc_ref.1) | copy-start | bytes 772

commit v2 on v1

--- a/solution.py
+++ b/solution.py
@@ -22,11 +22,11 @@
 
 
 def kernel(
-    geometry, grad_hbm, inner_ref, len_ref, off_ref, inc_ref,
+    geometry, grad_hbm, inner_hbm, len_hbm, off_ref, inc_hbm,
     out_ref, norm_ref,
-    grad, lhs, last_out, first_out, last_in, first_in, last_far, first_far,
+    grad, inner_ref, len_ref, inc_ref, lhs, last_out, first_out, last_in, first_in, last_far, first_far,
     terms_out, terms_in, clipped, send_1, recv_1, send_2, recv_2, send_3, recv_3,
-    load_sem, halo_send, halo_recv, terms_send, terms_recv,
+    load_sem, small_sem, halo_send, halo_recv, terms_send, terms_recv,
     send_sem_1, recv_sem_1, send_sem_2, recv_sem_2, send_sem_3, recv_sem_3,
 ):
     n_dp, n_z, n_x, n_y = geometry
@@ -54,6 +54,12 @@
     def in_y(other):
         return (dp, z * (n_x * n_y) + x * n_y + other)
 
+    smalls = []
+    for i, (hbm, ref) in enumerate(
+        ((len_hbm, len_ref), (inner_hbm, inner_ref), (inc_hbm, inc_ref))
+    ):
+        smalls.append(pltpu.make_async_copy(hbm, ref, small_sem.at[i]))
+        smalls[-1].start()
     loads = []
     for p in range(PARTS):
         columns = pl.ds(p * part, part)
@@ -77,6 +83,8 @@
             )
             greeted += 1
 
+    for copy in smalls:
+        copy.wait()
     lengths = len_ref[...].astype(F32)
     down = lax.broadcasted_iota(jnp.int32, (docs, docs), 0)
     across = lax.broadcasted_iota(jnp.int32, (docs, docs), 1)
@@ -113,10 +121,14 @@
     local = ids - first
     local = jnp.where(local < 0.0, local + docs, local)
     lhs[0:rank, :] = jnp.where(ids == last, inner, 0.0).astype(BF16)
-    for q in range(LOCAL_DOCS):
-        lhs[(q + 1) * rank : (q + 2) * rank, :] = jnp.where(local == float(q), inner, 0.0).astype(
-            BF16
-        )
+
+    def select_docs(begin, end):
+        for q in range(begin, end):
+            lhs[(q + 1) * rank : (q + 2) * rank, :] = jnp.where(
+                local == float(q), inner, 0.0
+            ).astype(BF16)
+
+    select_docs(0, 1)
 
     def halo(p):
         columns = pl.ds(p * part, part)
@@ -142,12 +154,12 @@
         ]
 
     doc_rows = LOCAL_DOCS * rank
-    squares = jnp.zeros((doc_rows, 128), F32)
+    squares_first = jnp.zeros((rank, 128), F32)
     halos = []
     for p in range(PARTS):
         loads[p].wait()
         columns = slice(p * part, (p + 1) * part)
-        sums = jnp.dot(lhs[...], grad[:, columns], preferred_element_type=F32)
+        sums = jnp.dot(lhs[0 : 2 * rank, :], grad[:, columns], preferred_element_type=F32)
         last_out[:, columns] = sums[0:rank].astype(BF16)
         first_out[:, columns] = sums[rank : 2 * rank].astype(BF16)
         if p == 0:
@@ -155,8 +167,16 @@
         halos.append(halo(p))
         for copy in halos[-1]:
             copy.start()
-        for tile in lane_tiles(sums[rank:]):
+        for tile in lane_tiles(sums[rank : 2 * rank]):
+            squares_first = squares_first + tile * tile
+    select_docs(1, LOCAL_DOCS)
+    squares = jnp.zeros((doc_rows - rank, 128), F32)
+    for p in range(PARTS):
+        columns = slice(p * part, (p + 1) * part)
+        sums = jnp.dot(lhs[2 * rank :, :], grad[:, columns], preferred_element_type=F32)
+        for tile in lane_tiles(sums):
             squares = squares + tile * tile
+    squares = jnp.concatenate([squares_first, squares], axis=0)
 
     by_row = jnp.sum(squares, axis=1, keepdims=True)
     label = first + lax.shift_right_logical(
@@ -213,6 +233,19 @@
     for slot, copy in enumerate(news):
         copy.wait_recv()
         near = near + terms_in[slot, 0:1, :]
+    for step in range(1, n_x):
+        slot = len(news)
+        news.append(
+            pltpu.make_async_remote_copy(
+                src_ref=terms_out,
+                dst_ref=terms_in.at[slot],
+                send_sem=terms_send.at[slot],
+                recv_sem=terms_recv.at[slot],
+                device_id=in_group(dp * n_x + lax.rem(x + step, n_x)),
+                device_id_type=MESH,
+            )
+        )
+        news[-1].start()
 
     norms = jnp.sqrt(jnp.maximum(near[:, 0:docs], 0.0))
     factor = inc_ref[...].astype(F32) * CLIP_NORM / jnp.maximum(norms, CLIP_NORM)
@@ -220,20 +253,36 @@
     name = lax.broadcasted_iota(jnp.int32, (docs, 1), 0).astype(F32)
     token_factor = jnp.sum(jnp.where(ids == name, factor, 0.0), axis=0, keepdims=True)
     scaled = (token_factor * inner).astype(BF16)
-    for p in range(PARTS):
-        columns = slice(p * part, (p + 1) * part)
-        clipped[:, columns] = jnp.dot(scaled, grad[:, columns], preferred_element_type=F32)
 
     each = width // (n_dp * n_ctx)
     run = n_y * each
-    half = n_z * run
-    for g in range(n_group):
-        base = (g // n_x) * (n_ctx * each) + (g % n_x) * run
-        for k in range(n_z):
-            column = base + k * (n_x * run)
-            send_1[g, :, k * run : (k + 1) * run] = clipped[0:8, column : column + run]
-            send_1[g, :, half + k * run : half + (k + 1) * run] = clipped[8:16, column : column + run]
-        send_1[g, :, 2 * half : 2 * half + 128] = jnp.broadcast_to(terms, (8, 128))
+    slab = n_z * run
+    sent = []
+    for step in range(1, n_dp + 1):
+        to_dp = lax.rem(dp + step, n_dp)
+        columns = pl.ds(pl.multiple_of(to_dp * (n_x * slab), 128), n_x * slab)
+        sums = jnp.dot(scaled, grad[:, columns], preferred_element_type=F32)
+        for other in range(n_x):
+            for k in range(n_z):
+                column = (k * n_x + other) * run
+                clipped[step - 1, other, :, k * run : (k + 1) * run] = sums[:, column : column + run]
+        for offset in range(1, n_x + 1):
+            if step == n_dp and offset == n_x:
+                continue
+            to_x = lax.rem(x + offset, n_x)
+            slot = len(sent)
+            send_1[slot, :, :] = clipped[step - 1, to_x].astype(BF16)
+            sent.append(
+                pltpu.make_async_remote_copy(
+                    src_ref=send_1.at[slot],
+                    dst_ref=recv_1.at[slot],
+                    send_sem=send_sem_1.at[slot],
+                    recv_sem=recv_sem_1.at[slot],
+                    device_id=in_group(to_dp * n_x + to_x),
+                    device_id_type=MESH,
+                )
+            )
+            sent[-1].start()
 
     def exchange(size, me, where, out, into, out_sem, in_sem):
         copies = []
@@ -263,34 +312,34 @@
             ).wait_recv()
         return copies
 
-    sent = exchange(n_group, group, in_group, send_1, recv_1, send_sem_1, recv_sem_1)
-    total = recv_1[0, :, 0 : 2 * half]
-    for g in range(1, n_group):
-        total = total + recv_1[g, :, 0 : 2 * half]
-    all_terms = recv_1[dp * n_x, :, 2 * half : 2 * half + 128]
-    for k in range(1, n_x):
-        all_terms = all_terms + recv_1[dp * n_x + k, :, 2 * half : 2 * half + 128]
+    all_terms = terms
+    for slot in range(2 * REACH, len(news)):
+        news[slot].wait_recv()
+        all_terms = all_terms + terms_in[slot, 0:1, :]
+    total = clipped[n_dp - 1, x, :, 0:slab]
+    for slot, copy in enumerate(sent):
+        copy.wait_recv()
+        total = total + recv_1[slot, :, 0:slab].astype(F32)
+    wide = send_2.shape[2]
     for k in range(n_z):
-        send_2[k, 0:8, 0:run] = total[:, k * run : (k + 1) * run]
-        send_2[k, 8:16, 0:run] = total[:, half + k * run : half + (k + 1) * run]
-        send_2[k, 16:24, :] = all_terms
+        send_2[k, :, 0:run] = total[0:8, k * run : (k + 1) * run]
+        send_2[k, :, run : 2 * run] = total[8:16, k * run : (k + 1) * run]
+        send_2[k, :, wide - docs :] = jnp.broadcast_to(all_terms[:, 0:docs], (8, docs))
     sent += exchange(n_z, z, in_z, send_2, recv_2, send_sem_2, recv_sem_2)
-    total = recv_2[0, 0:16, 0:run]
-    all_terms = recv_2[0, 16:24, :]
+    received = recv_2[0]
     for k in range(1, n_z):
-        total = total + recv_2[k, 0:16, 0:run]
-        all_terms = all_terms + recv_2[k, 16:24, :]
+        received = received + recv_2[k]
     for k in range(n_y):
-        send_3[k, 0:16, 0:each] = total[:, k * each : (k + 1) * each]
-        send_3[k, 16:24, :] = all_terms
+        send_3[k, :, 0:each] = received[:, k * each : (k + 1) * each]
+        send_3[k, :, each : 2 * each] = received[:, run + k * each : run + (k + 1) * each]
+        send_3[k, :, send_3.shape[2] - docs :] = received[:, wide - docs :]
     sent += exchange(n_y, y, in_y, send_3, recv_3, send_sem_3, recv_sem_3)
-    total = recv_3[0, 0:16, 0:each]
-    all_terms = recv_3[0, 16:17, 0:docs]
+    received = recv_3[0]
     for k in range(1, n_y):
-        total = total + recv_3[k, 0:16, 0:each]
-        all_terms = all_terms + recv_3[k, 16:17, 0:docs]
-    out_ref[...] = total
-    norm_ref[...] = jnp.sqrt(jnp.maximum(all_terms, 0.0))
+        received = received + recv_3[k]
+    out_ref[0:8, :] = received[:, 0:each]
+    out_ref[8:16, :] = received[:, each : 2 * each]
+    norm_ref[...] = jnp.sqrt(jnp.maximum(received[0:1, send_3.shape[2] - docs :], 0.0))
 
     for copies in halos:
         for copy in copies:
@@ -307,8 +356,11 @@
     docs = doc_lengths.shape[1]
     each = width // (n_dp * n_z * n_x * n_y)
     depth = (LOCAL_DOCS + 1) * rank
-    long = 2 * n_z * n_y * each + 128
+    long = pl.cdiv(n_z * n_y * each, 128) * 128
+    short = pl.cdiv(2 * each + docs, 128) * 128
+    wide = pl.cdiv(2 * n_y * each + docs, 128) * 128
     in_vmem = pl.BlockSpec(memory_space=pltpu.VMEM)
+    in_hbm = pl.BlockSpec(memory_space=pltpu.HBM)
     dma = pltpu.SemaphoreType.DMA
     gradient, norms = pl.pallas_call(
         functools.partial(kernel, geometry),
@@ -317,15 +369,18 @@
             jax.ShapeDtypeStruct((1, docs), F32),
         ),
         in_specs=[
-            pl.BlockSpec(memory_space=pl.ANY),
-            in_vmem,
-            in_vmem,
+            in_hbm,
+            in_hbm,
+            in_hbm,
             pl.BlockSpec(memory_space=pltpu.SMEM),
-            in_vmem,
+            in_hbm,
         ],
         out_specs=(in_vmem, in_vmem),
         scratch_shapes=[
             pltpu.VMEM((rows, width), BF16),
+            pltpu.VMEM((rank, rows), BF16),
+            pltpu.VMEM((1, docs), jnp.int32),
+            pltpu.VMEM((1, docs), jnp.int32),
             pltpu.VMEM((depth, rows), BF16),
             pltpu.VMEM((rank, width), BF16),
             pltpu.VMEM((rank, width), BF16),
@@ -334,28 +389,29 @@
             pltpu.VMEM((rank, width // 2), BF16),
             pltpu.VMEM((rank, width // 2), BF16),
             pltpu.VMEM((8, 128), F32),
-            pltpu.VMEM((2 * REACH, 8, 128), F32),
-            pltpu.VMEM((rank, width), F32),
-            pltpu.VMEM((n_group, 8, long), F32),
-            pltpu.VMEM((n_group, 8, long), F32),
-            pltpu.VMEM((n_z, 24, 128), F32),
-            pltpu.VMEM((n_z, 24, 128), F32),
-            pltpu.VMEM((n_y, 24, 128), F32),
-            pltpu.VMEM((n_y, 24, 128), F32),
+            pltpu.VMEM((2 * REACH + n_x - 1, 8, 128), F32),
+            pltpu.VMEM((n_dp, n_x, rank, long), F32),
+            pltpu.VMEM((n_group - 1, rank, long), BF16),
+            pltpu.VMEM((n_group - 1, rank, long), BF16),
+            pltpu.VMEM((n_z, 8, wide), F32),
+            pltpu.VMEM((n_z, 8, wide), F32),
+            pltpu.VMEM((n_y, 8, short), F32),
+            pltpu.VMEM((n_y, 8, short), F32),
             dma((PARTS,)),
+            dma((3,)),
             dma((PARTS, 3)),
             dma((PARTS, 3)),
-            dma((2 * REACH,)),
-            dma((2 * REACH,)),
-            dma((n_group,)),
-            dma((n_group,)),
+            dma((2 * REACH + n_x - 1,)),
+            dma((2 * REACH + n_x - 1,)),
+            dma((n_group - 1,)),
+            dma((n_group - 1,)),
             dma((n_z,)),
             dma((n_z,)),
             dma((n_y,)),
             dma((n_y,)),
         ],
         compiler_params=pltpu.CompilerParams(
-            collective_id=0, has_side_effects=True, vmem_limit_bytes=40 * 2**20
+            collective_id=0, has_side_effects=True, vmem_limit_bytes=60 * 2**20
         ),
     )(out_grad, adapter_inner.T, doc_lengths, slab_offset, included)
     return gradient.T, norms

time: 53.9 us -> 47.6 us (0.88)
  Pallas kernels: 46.9 us -> 43.6 us
  local copies, waits for them, and re-layouts: 5.54 us -> 2.51 us
    pallas_call x1, Pallas kernels: 46.9 us -> 43.6 us  [on_device(): pl.pallas_call(functools.partial(kernel, geometry), out_shape=(jax.ShapeD...]
    unnamed x10 -> x2, local copies, waits for them, and re-layouts: 5.54 us -> 2.51 us
where the time goes in v2:
time: 47.6 us; the launch traced here: 47.4 us
  Pallas kernels  43.6 us (92%)
  local copies, waits for them, and re-layouts  2.51 us (5%)
  between operations  1.29 us (3%)
    pallas_call x1, Pallas kernels, on_device(): pl.pallas_call(functools.partial(kernel, geometry), out_shape=(jax.ShapeD...  43.6 us
    unnamed x2, local copies, waits for them, and re-layouts  2.51 us

profile of v2, /device:TPU:1, one launch (start us, length us, event | category | flops | bytes accessed | tf_op | source)
XLA Modules:
  0.0 47.4 jit_solution(7766351110246798497)
XLA Ops:
  1.3 43.6 %shard_map.68 = (f32[16,9]{1,0:T(8,128)}, f32[1,64]{1,0:T(1,128)}) custom-call(bf16[512,4608]{1,0:T(8,128)(2,1)} %grad_hbm.1, bf16[16,512]{1,0:T(8,128)(2,1)} %bitcast.2, s32[1,64]{1,0:T(1,128)} %len_hbm.1, s32[1]{0:T(128)S(6)} %copy.9.off_ref, s32[1,64]{1,0:T(1,128)} %inc_hbm.1), custom_call_target="tpu_custom_call" | custom-call | tf_op jit(solution)/shard_map/pallas_call | solution.py:365
  44.9 1.4 %copy.7 = f32[9,16]{1,0:T(8,128)} copy(f32[9,16]{0,1:T(8,128)} %bitcast.3) | data formatting | bytes 1152
  46.3 1.1 %copy.10 = f32[1,64]{1,0:T(1,128)} copy(f32[1,64]{1,0:T(1,128)} %get-tuple-element.11) | data formatting | bytes 512

commit v3 on v2

--- a/solution.py
+++ b/solution.py
@@ -130,48 +130,56 @@
 
     select_docs(0, 1)
 
-    def halo(p):
+    low = range(PARTS // 2)
+    high = range(PARTS // 2, PARTS)
+
+    def move(kind, p):
         columns = pl.ds(p * part, part)
         far = pl.ds((p % (PARTS // 2)) * part, part)
-        low = p < PARTS // 2
-        moves = [
-            (last_out.at[:, columns], last_in.at[:, columns], along(1)),
-            (first_out.at[:, columns], first_in.at[:, columns], along(-1)),
-            (last_out.at[:, columns], last_far.at[:, far], along(2))
-            if low
-            else (first_out.at[:, columns], first_far.at[:, far], along(-2)),
-        ]
-        return [
-            pltpu.make_async_remote_copy(
-                src_ref=src,
-                dst_ref=dst,
-                send_sem=halo_send.at[p, i],
-                recv_sem=halo_recv.at[p, i],
-                device_id=to,
-                device_id_type=MESH,
-            )
-            for i, (src, dst, to) in enumerate(moves)
-        ]
+        src, dst, to = {
+            "last": (last_out.at[:, columns], last_in.at[:, columns], along(1)),
+            "first": (first_out.at[:, columns], first_in.at[:, columns], along(-1)),
+            "on": (last_in.at[:, columns], last_far.at[:, far], along(1))
+            if p in low
+            else (first_in.at[:, columns], first_far.at[:, far], along(-1)),
+        }[kind]
+        slot = ("last", "first", "on").index(kind)
+        return pltpu.make_async_remote_copy(
+            src_ref=src,
+            dst_ref=dst,
+            send_sem=halo_send.at[p, slot],
+            recv_sem=halo_recv.at[p, slot],
+            device_id=to,
+            device_id_type=MESH,
+        )
 
     doc_rows = LOCAL_DOCS * rank
     squares_first = jnp.zeros((rank, 128), F32)
-    halos = []
-    for p in range(PARTS):
+    halos = {(kind, p): move(kind, p) for kind in ("last", "first", "on") for p in range(PARTS)}
+    begun = 0
+    for p in [q for pair in zip(low, high) for q in pair]:
         loads[p].wait()
         columns = slice(p * part, (p + 1) * part)
         sums = jnp.dot(lhs[0 : 2 * rank, :], grad[:, columns], preferred_element_type=F32)
         last_out[:, columns] = sums[0:rank].astype(BF16)
         first_out[:, columns] = sums[rank : 2 * rank].astype(BF16)
-        if p == 0:
+        if begun == 0:
             pl.semaphore_wait(barrier, greeted)
-        halos.append(halo(p))
-        for copy in halos[-1]:
-            copy.start()
+        begun += 1
+        halos["last" if p in low else "first", p].start()
         for tile in lane_tiles(sums[rank : 2 * rank]):
             squares_first = squares_first + tile * tile
+    for p, q in zip(low, high):
+        halos["first", p].start()
+        halos["last", q].start()
     select_docs(1, LOCAL_DOCS)
     squares = jnp.zeros((doc_rows - rank, 128), F32)
     for p in range(PARTS):
+        if p >= PARTS // 2:
+            halos["last", p - PARTS // 2].wait_recv()
+            halos["on", p - PARTS // 2].start()
+            halos["first", p].wait_recv()
+            halos["on", p].start()
         columns = slice(p * part, (p + 1) * part)
         sums = jnp.dot(lhs[2 * rank :, :], grad[:, columns], preferred_element_type=F32)
         for tile in lane_tiles(sums):
@@ -197,12 +205,12 @@
     for p in range(PARTS):
         columns = slice(p * part, (p + 1) * part)
         far = slice((p % (PARTS // 2)) * part, (p % (PARTS // 2) + 1) * part)
-        for copy in halos[p]:
-            copy.wait_recv()
+        halos["first" if p in low else "last", p].wait_recv()
+        halos["on", p].wait_recv()
         from_behind = last_in[:, columns].astype(F32)
         from_ahead = first_in[:, columns].astype(F32)
         partner = pair_1 * first_out[:, columns].astype(F32) + pair_2 * from_ahead
-        if p < PARTS // 2:
+        if p in low:
             product = from_behind * partner + (pair_3_behind * from_ahead) * last_far[
                 :, far
             ].astype(F32)
@@ -341,10 +349,7 @@
     out_ref[8:16, :] = received[:, each : 2 * each]
     norm_ref[...] = jnp.sqrt(jnp.maximum(received[0:1, send_3.shape[2] - docs :], 0.0))
 
-    for copies in halos:
-        for copy in copies:
-            copy.wait_send()
-    for copy in news + sent:
+    for copy in [*halos.values(), *news, *sent]:
         copy.wait_send()
 
 

time: 47.6 us -> 50.5 us (1.061)
  Pallas kernels: 43.6 us -> 46.4 us
    pallas_call x1, Pallas kernels: 43.6 us -> 46.4 us  [on_device(): pl.pallas_call(functools.partial(kernel, geometry), out_shape=(jax.ShapeD...]
where the time goes in v3:
time: 50.5 us; the launch traced here: 50.2 us
  Pallas kernels  46.4 us (92%)
  local copies, waits for them, and re-layouts  2.51 us (5%)
  between operations  1.29 us (3%)
    pallas_call x1, Pallas kernels, on_device(): pl.pallas_call(functools.partial(kernel, geometry), out_shape=(jax.ShapeD...  46.4 us
    unnamed x2, local copies, waits for them, and re-layouts  2.51 us

profile of v3, /device:TPU:1, one launch (start us, length us, event | category | flops | bytes accessed | tf_op | source)
XLA Modules:
  0.0 50.2 jit_solution(15121766427862496157)
XLA Ops:
  1.3 46.4 %shard_map.68 = (f32[16,9]{1,0:T(8,128)}, f32[1,64]{1,0:T(1,128)}) custom-call(bf16[512,4608]{1,0:T(8,128)(2,1)} %grad_hbm.1, bf16[16,512]{1,0:T(8,128)(2,1)} %bitcast.2, s32[1,64]{1,0:T(1,128)} %len_hbm.1, s32[1]{0:T(128)S(6)} %copy.9.off_ref, s32[1,64]{1,0:T(1,128)} %inc_hbm.1), custom_call_target="tpu_custom_call" | custom-call | tf_op jit(solution)/shard_map/pallas_call | solution.py:370
  47.7 1.4 %copy.7 = f32[9,16]{1,0:T(8,128)} copy(f32[9,16]{0,1:T(8,128)} %bitcast.3) | data formatting | bytes 1152
  49.1 1.1 %copy.10 = f32[1,64]{1,0:T(1,128)} copy(f32[1,64]{1,0:T(1,128)} %get-tuple-element.11) | data formatting | bytes 512

commit v4 on v2

--- a/solution.py
+++ b/solution.py
@@ -12,6 +12,7 @@
 LOCAL_DOCS = 23
 REACH = 3
 PARTS = 4
+STRIP = 512
 MESH = pl.DeviceIdType.MESH
 F32 = jnp.float32
 BF16 = jnp.bfloat16
@@ -170,12 +171,16 @@
         for tile in lane_tiles(sums[rank : 2 * rank]):
             squares_first = squares_first + tile * tile
     select_docs(1, LOCAL_DOCS)
-    squares = jnp.zeros((doc_rows - rank, 128), F32)
-    for p in range(PARTS):
-        columns = slice(p * part, (p + 1) * part)
+
+    def add_squares(i, squares):
+        columns = pl.ds(pl.multiple_of(i * STRIP, 128), STRIP)
         sums = jnp.dot(lhs[2 * rank :, :], grad[:, columns], preferred_element_type=F32)
         for tile in lane_tiles(sums):
             squares = squares + tile * tile
+        return squares
+
+    squares = jnp.zeros((doc_rows - rank, 128), F32)
+    squares = lax.fori_loop(0, width // STRIP, add_squares, squares)
     squares = jnp.concatenate([squares_first, squares], axis=0)
 
     by_row = jnp.sum(squares, axis=1, keepdims=True)
@@ -257,32 +262,43 @@
     each = width // (n_dp * n_ctx)
     run = n_y * each
     slab = n_z * run
-    sent = []
-    for step in range(1, n_dp + 1):
+
+    def share(step, offset):
+        slot = (step - 1) * n_x + offset - 1
+        to = lax.rem(dp + step, n_dp) * n_x + lax.rem(x + offset, n_x)
+        return pltpu.make_async_remote_copy(
+            src_ref=send_1.at[slot],
+            dst_ref=recv_1.at[slot],
+            send_sem=send_sem_1.at[slot],
+            recv_sem=recv_sem_1.at[slot],
+            device_id=in_group(to),
+            device_id_type=MESH,
+        )
+
+    def multiply(step, offsets):
         to_dp = lax.rem(dp + step, n_dp)
         columns = pl.ds(pl.multiple_of(to_dp * (n_x * slab), 128), n_x * slab)
         sums = jnp.dot(scaled, grad[:, columns], preferred_element_type=F32)
         for other in range(n_x):
             for k in range(n_z):
                 column = (k * n_x + other) * run
-                clipped[step - 1, other, :, k * run : (k + 1) * run] = sums[:, column : column + run]
-        for offset in range(1, n_x + 1):
-            if step == n_dp and offset == n_x:
-                continue
-            to_x = lax.rem(x + offset, n_x)
-            slot = len(sent)
-            send_1[slot, :, :] = clipped[step - 1, to_x].astype(BF16)
-            sent.append(
-                pltpu.make_async_remote_copy(
-                    src_ref=send_1.at[slot],
-                    dst_ref=recv_1.at[slot],
-                    send_sem=send_sem_1.at[slot],
-                    recv_sem=recv_sem_1.at[slot],
-                    device_id=in_group(to_dp * n_x + to_x),
-                    device_id_type=MESH,
-                )
-            )
-            sent[-1].start()
+                clipped[other, :, k * run : (k + 1) * run] = sums[:, column : column + run]
+        for offset in offsets:
+            slot = (step - 1) * n_x + offset - 1
+            send_1[slot] = clipped[lax.rem(x + offset, n_x)].astype(BF16)
+            share(step, offset).start()
+
+    @pl.loop(1, n_dp)
+    def _(step):
+        multiply(step, range(1, n_x + 1))
+
+    multiply(n_dp, range(1, n_x))
+    sent = [
+        share(step, offset)
+        for step in range(1, n_dp + 1)
+        for offset in range(1, n_x + 1)
+        if (step, offset) != (n_dp, n_x)
+    ]
 
     def exchange(size, me, where, out, into, out_sem, in_sem):
         copies = []
@@ -316,7 +332,7 @@
     for slot in range(2 * REACH, len(news)):
         news[slot].wait_recv()
         all_terms = all_terms + terms_in[slot, 0:1, :]
-    total = clipped[n_dp - 1, x, :, 0:slab]
+    total = clipped[x, :, 0:slab]
     for slot, copy in enumerate(sent):
         copy.wait_recv()
         total = total + recv_1[slot, :, 0:slab].astype(F32)
@@ -390,7 +406,7 @@
             pltpu.VMEM((rank, width // 2), BF16),
             pltpu.VMEM((8, 128), F32),
             pltpu.VMEM((2 * REACH + n_x - 1, 8, 128), F32),
-            pltpu.VMEM((n_dp, n_x, rank, long), F32),
+            pltpu.VMEM((n_x, rank, long), F32),
             pltpu.VMEM((n_group - 1, rank, long), BF16),
             pltpu.VMEM((n_group - 1, rank, long), BF16),
             pltpu.VMEM((n_z, 8, wide), F32),

time: 47.6 us -> 47.7 us (level)
  no operation moved by 1% of the time
where the time goes in v4:
time: 47.7 us; the launch traced here: 47.5 us
  Pallas kernels  43.7 us (92%)
  local copies, waits for them, and re-layouts  2.51 us (5%)
  between operations  1.29 us (3%)
    pallas_call x1, Pallas kernels, on_device(): pl.pallas_call(functools.partial(kernel, geometry), out_shape=(jax.ShapeD...  43.7 us
    unnamed x2, local copies, waits for them, and re-layouts  2.51 us

profile of v4, /device:TPU:1, one launch (start us, length us, event | category | flops | bytes accessed | tf_op | source)
XLA Modules:
  0.0 47.5 jit_solution(13514103718656152929)
XLA Ops:
  1.3 43.7 %shard_map.68 = (f32[16,9]{1,0:T(8,128)}, f32[1,64]{1,0:T(1,128)}) custom-call(bf16[512,4608]{1,0:T(8,128)(2,1)} %grad_hbm.1, bf16[16,512]{1,0:T(8,128)(2,1)} %bitcast.2, s32[1,64]{1,0:T(1,128)} %len_hbm.1, s32[1]{0:T(128)S(6)} %copy.9.off_ref, s32[1,64]{1,0:T(1,128)} %inc_hbm.1), custom_call_target="tpu_custom_call" | custom-call | tf_op jit(solution)/shard_map/pallas_call | solution.py:381
  45.0 1.4 %copy.7 = f32[9,16]{1,0:T(8,128)} copy(f32[9,16]{0,1:T(8,128)} %bitcast.3) | data formatting | bytes 1152
  46.3 1.1 %copy.10 = f32[1,64]{1,0:T(1,128)} copy(f32[1,64]{1,0:T(1,128)} %get-tuple-element.11) | data formatting | bytes 512

commit v5 on v4

--- a/solution.py
+++ b/solution.py
@@ -166,7 +166,7 @@
         if p == 0:
             pl.semaphore_wait(barrier, greeted)
         halos.append(halo(p))
-        for copy in halos[-1]:
+        for copy in reversed(halos[-1]):
             copy.start()
         for tile in lane_tiles(sums[rank : 2 * rank]):
             squares_first = squares_first + tile * tile

time: 47.7 us -> 47.6 us (level)
  no operation moved by 1% of the time
where the time goes in v5:
time: 47.6 us; the launch traced here: 47.4 us
  Pallas kernels  43.6 us (92%)
  local copies, waits for them, and re-layouts  2.51 us (5%)
  between operations  1.29 us (3%)
    pallas_call x1, Pallas kernels, on_device(): pl.pallas_call(functools.partial(kernel, geometry), out_shape=(jax.ShapeD...  43.6 us
    unnamed x2, local copies, waits for them, and re-layouts  2.51 us

profile of v5, /device:TPU:1, one launch (start us, length us, event | category | flops | bytes accessed | tf_op | source)
XLA Modules:
  0.0 47.4 jit_solution(12155618624041578447)
XLA Ops:
  1.3 43.6 %shard_map.68 = (f32[16,9]{1,0:T(8,128)}, f32[1,64]{1,0:T(1,128)}) custom-call(bf16[512,4608]{1,0:T(8,128)(2,1)} %grad_hbm.1, bf16[16,512]{1,0:T(8,128)(2,1)} %bitcast.2, s32[1,64]{1,0:T(1,128)} %len_hbm.1, s32[1]{0:T(128)S(6)} %copy.9.off_ref, s32[1,64]{1,0:T(1,128)} %inc_hbm.1), custom_call_target="tpu_custom_call" | custom-call | tf_op jit(solution)/shard_map/pallas_call | solution.py:381
  44.9 1.4 %copy.7 = f32[9,16]{1,0:T(8,128)} copy(f32[9,16]{0,1:T(8,128)} %bitcast.3) | data formatting | bytes 1152
  46.3 1.1 %copy.10 = f32[1,64]{1,0:T(1,128)} copy(f32[1,64]{1,0:T(1,128)} %get-tuple-element.11) | data formatting | bytes 512

commit v6 on v5

--- a/solution.py
+++ b/solution.py
@@ -220,7 +220,7 @@
 
     terms_out[...] = jnp.broadcast_to(terms, (8, 128))
     news = []
-    for distance in range(1, REACH + 1):
+    for distance in range(REACH, 0, -1):
         for sign in (1, -1):
             slot = len(news)
             news.append(
@@ -302,7 +302,7 @@
 
     def exchange(size, me, where, out, into, out_sem, in_sem):
         copies = []
-        for step in range(1, size):
+        for step in sorted(range(1, size), key=lambda k: -min(k, size - k)):
             to = lax.rem(me + step, size)
             copies.append(
                 pltpu.make_async_remote_copy(

time: 47.6 us -> 47.4 us (level)
  no operation moved by 1% of the time
where the time goes in v6:
time: 47.4 us; the launch traced here: 47.2 us
  Pallas kernels  43.4 us (92%)
  local copies, waits for them, and re-layouts  2.51 us (5%)
  between operations  1.29 us (3%)
    pallas_call x1, Pallas kernels, on_device(): pl.pallas_call(functools.partial(kernel, geometry), out_shape=(jax.ShapeD...  43.4 us
    unnamed x2, local copies, waits for them, and re-layouts  2.51 us

profile of v6, /device:TPU:1, one launch (start us, length us, event | category | flops | bytes accessed | tf_op | source)
XLA Modules:
  0.0 47.2 jit_solution(9072530761136081471)
XLA Ops:
  1.3 43.4 %shard_map.68 = (f32[16,9]{1,0:T(8,128)}, f32[1,64]{1,0:T(1,128)}) custom-call(bf16[512,4608]{1,0:T(8,128)(2,1)} %grad_hbm.1, bf16[16,512]{1,0:T(8,128)(2,1)} %bitcast.2, s32[1,64]{1,0:T(1,128)} %len_hbm.1, s32[1]{0:T(128)S(6)} %copy.9.off_ref, s32[1,64]{1,0:T(1,128)} %inc_hbm.1), custom_call_target="tpu_custom_call" | custom-call | tf_op jit(solution)/shard_map/pallas_call | solution.py:381
  44.7 1.4 %copy.7 = f32[9,16]{1,0:T(8,128)} copy(f32[9,16]{0,1:T(8,128)} %bitcast.3) | data formatting | bytes 1152
  46.1 1.1 %copy.10 = f32[1,64]{1,0:T(1,128)} copy(f32[1,64]{1,0:T(1,128)} %get-tuple-element.11) | data formatting | bytes 512
